TPU v7x, 32 devices: a whole 2x2x4 slice. The times are simulated.
32 devices in a mesh: pipe: 4 (over z), dp: 8 (over y, x, core).
Axes of the slice: x: 2, y: 2, z: 4, core: 2. Of those that a mesh axis runs over, the one named last changes fastest.
Arguments:
- section_inputs: bfloat16 [4096, 6144], P(('pipe', 'dp')), may hold values from -6 to 6
- out_grad: bfloat16 [1024, 6144], P('dp'), may hold values from -6 to 6
- up_weight: bfloat16 [512, 6144], P('pipe'), may hold values from -0.078125 to 0.078125
- down_weight: bfloat16 [512, 6144], P('pipe'), may hold values from -0.078125 to 0.078125
- momentum: bfloat16 [1024, 6144], P('pipe'), may hold values from -4 to 4
- worker_error: bfloat16 [1024, 49152], P('pipe', 'dp'), may hold values from -4 to 4
- server_error: float32 [1024, 6144], P('pipe', 'dp'), may hold values from -3 to 3
- owner_map: int32 [8], replicated, may hold values from 0 to 7, each once
Outputs:
- new_momentum: bfloat16 [1024, 6144], P('pipe')
- new_worker_error: bfloat16 [1024, 49152], P('pipe', 'dp')
- new_server_error: float32 [1024, 6144], P('pipe', 'dp')
Inputs may be any that keep to these rules, and one draw needn't show every extreme that they name: owner_map names every worker exactly once.
All inputs are finite; a program needn't handle non-finite values. Where the computation divides by a largest or mean magnitude, that divisor is 1e-20 or more.
Results may differ from a plain program's by a relative error of at most 0.0085.
Values may be sent and summed in bfloat16 or wider, within the bound.
A program may use at most 128 MiB of HBM per device.

v0:
```python
import jax
import jax.numpy as jnp
from jax import lax
from jax.sharding import PartitionSpec as P

epsilon = 1e-06


def passed_along(block, axis, distance):
    devices = range(lax.axis_size(axis))
    route = [(i - distance, i) for i in devices if i - distance in devices]
    return lax.ppermute(block, axis, route)


def gelu_parts(pre_act):
    activated, pullback = jax.vjp(jax.nn.gelu, pre_act)
    gelu_slope = pullback(jnp.ones_like(pre_act))[0]
    return (activated, gelu_slope)


def backstep(incoming, slope_rows, up_weight, down_weight):
    contract = (((1,), (1,)), ((), ()))
    d_act = lax.dot_general(incoming, down_weight, contract, preferred_element_type=jnp.float32)
    d_pre = (d_act * slope_rows).astype(jnp.bfloat16)
    passed = (
        incoming.astype(jnp.float32) + jnp.dot(d_pre, up_weight, preferred_element_type=jnp.float32)
    ).astype(jnp.bfloat16)
    return (d_pre, passed)


def on_device(
    section_inputs,
    out_grad,
    up_weight,
    down_weight,
    momentum,
    worker_error,
    server_error,
    owner_map,
):
    sections = lax.axis_size("pipe")
    section = lax.axis_index("pipe")
    ranks = lax.axis_size("dp")
    tok_rows = section_inputs.shape[0]
    hidden_units = up_weight.shape[0]
    contract = (((1,), (1,)), ((), ()))
    pre_act = lax.dot_general(
        section_inputs, up_weight, contract, preferred_element_type=jnp.float32
    )
    activated, gelu_slope = gelu_parts(pre_act)
    act_b = activated.astype(jnp.bfloat16)
    kept_grad = jnp.zeros_like(out_grad)
    kept_pre = jnp.zeros((tok_rows, hidden_units), jnp.bfloat16)
    incoming = out_grad
    passed = out_grad
    for turn_number in range(sections):
        if turn_number > 0:
            incoming = passed_along(passed, "pipe", -1)
        d_pre, passed = backstep(incoming, gelu_slope, up_weight, down_weight)
        is_active = section == sections - 1 - turn_number
        kept_grad = jnp.where(is_active, incoming, kept_grad)
        kept_pre = jnp.where(is_active, d_pre, kept_pre)
    token_contract = (((0,), (0,)), ((), ()))
    grad_up = lax.dot_general(
        kept_pre, section_inputs, token_contract, preferred_element_type=jnp.float32
    )
    grad_down = lax.dot_general(
        act_b, kept_grad, token_contract, preferred_element_type=jnp.float32
    )
    weight_grads = jnp.concatenate([grad_up, grad_down], axis=0)
    combined = (
        0.9 * momentum.astype(jnp.float32) + 0.1 * weight_grads + worker_error.astype(jnp.float32)
    )
    param_rows = combined.shape[0]
    group_cols = combined.shape[1] // ranks
    blocks = combined.reshape(param_rows, ranks, group_cols)
    group_scale = jnp.mean(jnp.abs(blocks), axis=(0, 2), keepdims=True) + epsilon
    packed = (group_scale * jnp.tanh(blocks / group_scale)).astype(jnp.bfloat16)
    new_worker = (
        (blocks - packed.astype(jnp.float32))
        .astype(jnp.bfloat16)
        .reshape(param_rows, ranks * group_cols)
    )
    rank_group = jnp.argsort(owner_map)
    outgoing = jnp.take(packed, rank_group, axis=1)
    received = lax.all_to_all(outgoing, "dp", split_axis=1, concat_axis=1, tiled=True)
    average = jnp.sum(received.astype(jnp.float32), axis=1) / ranks
    updated = average + server_error
    server_scale = jnp.mean(jnp.abs(updated)) + epsilon
    server_packed = (server_scale * jnp.tanh(updated / server_scale)).astype(jnp.bfloat16)
    new_server = updated - server_packed.astype(jnp.float32)
    collected = lax.all_gather(server_packed[:, None, :], "dp", axis=1, tiled=True)
    new_momentum = jnp.take(collected, owner_map, axis=1).reshape(param_rows, ranks * group_cols)
    return (new_momentum, new_worker, new_server)


def solution(mesh):
    in_specs = (
        P(("pipe", "dp"), None),
        P("dp", None),
        P("pipe", None),
        P("pipe", None),
        P("pipe", None),
        P("pipe", "dp"),
        P("pipe", "dp"),
        P(),
    )
    out_specs = (P("pipe", None), P("pipe", "dp"), P("pipe", "dp"))
    return jax.shard_map(
        on_device, mesh=mesh, in_specs=in_specs, out_specs=out_specs, check_vma=False
    )
```

profile of v0, /device:TPU:1, one launch (start us, length us, event | category | flops | bytes accessed | tf_op | source)
XLA Modules:
  0.0 266.7 jit_solution(7359632600641126229)
XLA Ops:
  7.2 1.3 copy-done
  8.6 2.1 fusion.48
  10.7 0.6 fusion.15
  11.3 0.6 fusion
  11.9 1.3 collective-permute-start
  13.2 36.8 %collective-permute-done = bf16[128,6144]{1,0:T(8,128)(2,1)S(1)} collective-permute-done((bf16[128,6144]{1,0:T(8,128)(2,1)S(1)}, bf16[128,6144]{1,0:T(8,128)(2,1)S(1)}, u32[]{:S(2)}, u32[]{:S(2)}) %collective-permute-start) | collective-permute-done | bytes 1572896 | tf_op jit(solution)/shard_map/ppermute | solution.py:12
  50.0 0.6 fusion.16
  50.6 0.6 add_convert_fusion.1
  51.2 1.3 collective-permute-start.1
  52.5 35.2 %collective-permute-done.1 = bf16[128,6144]{1,0:T(8,128)(2,1)S(1)} collective-permute-done((bf16[128,6144]{1,0:T(8,128)(2,1)S(1)}, bf16[128,6144]{1,0:T(8,128)(2,1)S(1)}, u32[]{:S(2)}, u32[]{:S(2)}) %collective-permute-start.1) | collective-permute-done | bytes 1572896 | tf_op jit(solution)/shard_map/ppermute | solution.py:12
  88.3 1.7 add_convert_fusion
  90.1 1.3 collective-permute-start.2
  91.4 1.0 sort.17
  92.4 33.6 %collective-permute-done.2 = bf16[128,6144]{1,0:T(8,128)(2,1)} collective-permute-done((bf16[128,6144]{1,0:T(8,128)(2,1)}, bf16[128,6144]{1,0:T(8,128)(2,1)}, u32[]{:S(2)}, u32[]{:S(2)}) %collective-permute-start.2) | collective-permute-done | bytes 1572896 | tf_op jit(solution)/shard_map/ppermute | solution.py:12
  126.0 3.9 %fusion.6 = f32[128,6144]{1,0:T(8,128)} fusion(bf16[128,6144]{1,0:T(8,128)(2,1)} %collective-permute-done.2, bf16[128,6144]{1,0:T(8,128)(2,1)} %copy-done.5, bf16[128,6144]{1,0:T(8,128)(2,1)} %copy-done.4, bf16[128,6144]{1,0:T(8,128)(2,1)} %param.11, pred[]{:T(512)S(6)} %eq.15, pred[]{:T(512)S(6)} %eq.14, pred[]{:T(512)S(6)} %eq.13, pred[]{:T(512)S(6)} %eq.12, ...), kind=kOutput, calls=%fused_computation.19 | convolution fusion | flops 204619776 | bytes 9502724 | tf_op jit(solution)/shard_map/dot_general | solution.py:67
  129.9 5.0 %fusion.20 = f32[128,6144]{1,0:T(8,128)} fusion(bf16[128,6144]{1,0:T(8,128)(2,1)S(1)} %copy-done.6, bf16[128,6144]{1,0:T(8,128)(2,1)} %collective-permute-done.2, bf16[128,6144]{1,0:T(8,128)(2,1)S(1)} %copy-done.2, bf16[128,128]{1,0:T(8,128)(2,1)S(1)} %fusion.17, bf16[128,128]{1,0:T(8,128)(2,1)S(1)} %fusion.16, bf16[128,128]{1,0:T(8,128)(2,1)S(1)} %fusion.15, ...), kind=kOutput, calls=%fused_computation.37 | convolution fusion | flops 403030016 | bytes 8028164 | tf_op jit(solution)/shard_map/dot_general | solution.py:64
  134.9 7.2 %abs_reduce_fusion = (f32[6144]{0:T(1024)S(1)}, f32[256,6144]{1,0:T(8,128)}) fusion(bf16[256,6144]{1,0:T(8,128)(2,1)} %param.15, f32[128,6144]{1,0:T(8,128)} %fusion.6, f32[128,6144]{1,0:T(8,128)} %fusion.20, bf16[256,6144]{1,0:T(8,128)(2,1)} %param.14), kind=kLoop, calls=%fused_computation.14 | loop fusion | flops 14149632 | bytes 18898944 | tf_op jit(solution)/shard_map/reduce_sum | solution.py:77
  142.3 5.8 %fusion.3 = bf16[256,8,768]{2,0,1:T(8,128)(2,1)} fusion(f32[32,8,8,768]{3,2,1,0:T(8,128)} %bitcast.32, f32[8]{0:T(128)S(1)} %multiply_add_fusion.1), kind=kLoop, calls=%fused_computation.7 | loop fusion | flops 4718592 | bytes 9437216 | tf_op jit(solution)/shard_map/convert_element_type | solution.py:78
  148.1 4.3 %gather_fusion = bf16[8,256,768]{2,1,0:T(8,128)(2,1)} fusion(bf16[256,8,768]{2,0,1:T(8,128)(2,1)} %fusion.3, s32[1024]{0:T(1024)S(1)} %pad_clamp_fusion.1), kind=kCustom, calls=%fused_computation.clone | custom fusion | bytes 6291488 | tf_op jit(solution)/shard_map/jit(_take)/gather | solution.py:85
  152.4 2.3 select_bitcast_fusion.1
  154.6 42.6 %all_to_all.5 = bf16[256,8,768]{2,0,1:T(8,128)(2,1)S(1)} all-to-all(bf16[256,8,768]{2,0,1:T(8,128)(2,1)S(1)} %select_bitcast_fusion.1), channel_id=1, replica_groups=mesh['pipe'=4,'dp'=8] {'dp'}, dimensions={1} | all-to-all | bytes 6291456 | tf_op jit(solution)/shard_map/all_to_all | solution.py:86
  197.7 0.7 copy-done.7
  198.4 0.8 abs_reduce_fusion.1
  199.9 1.2 convert_subtract_fusion
  201.2 5.6 %subtract_convert_fusion = bf16[256,6144]{1,0:T(8,128)(2,1)} fusion(f32[256,6144]{1,0:T(8,128)} %get-tuple-element.16, f32[6144]{0:T(1024)S(1)} %mul.111), kind=kLoop, calls=%fused_computation.11 | loop fusion | flops 9437184 | bytes 9461760 | tf_op jit(solution)/shard_map/convert_element_type | solution.py:81
  206.8 26.2 %all-gather.3.cloned.1.call-done = bf16[256,6144]{1,0:T(8,128)(2,1)} async-done(((bf16[256,768]{1,0:T(8,128)(2,1)}), bf16[256,6144]{1,0:T(8,128)(2,1)}) %all-gather.3.cloned.1.call-update) | async-done | bytes 3145744 | tf_op jit(solution)/shard_map/all_gather | solution.py:92
  232.9 4.6 %copy.24 = bf16[256,6144]{0,1:T(8,128)(2,1)} copy(bf16[256,6144]{1,0:T(8,128)(2,1)} %all-gather.3.cloned.1.call-done) | data formatting | bytes 6291456 | tf_op jit(solution)/shard_map/all_gather | solution.py:92
  237.6 4.6 %copy.25 = bf16[256,8,768]{2,0,1:T(8,128)(2,1)} copy(bf16[256,8,768]{0,2,1:T(8,128)(2,1)} %bitcast.33) | data formatting | bytes 6291456 | tf_op jit(solution)/shard_map/all_gather | solution.py:92
  242.2 4.3 %gather_fusion.1 = bf16[8,256,768]{2,1,0:T(8,128)(2,1)} fusion(bf16[256,8,768]{2,0,1:T(8,128)(2,1)} %copy.25, s32[1024]{0:T(1024)S(1)} %pad_clamp_fusion), kind=kCustom, calls=%fused_computation.1.clone | custom fusion | bytes 6291488 | tf_op jit(solution)/shard_map/jit(_take)/gather | solution.py:93
  246.5 3.9 %select_bitcast_fusion = bf16[256,8,768]{2,0,1:T(8,128)(2,1)} fusion(bf16[8,256,768]{2,1,0:T(8,128)(2,1)} %gather_fusion.1, pred[8]{0:T(512)(128)(4,1)S(1)} %compare_and_fusion), kind=kLoop, calls=%fused_computation.15 | loop fusion | flops 1572864 | bytes 6291464 | tf_op jit(solution)/shard_map/jit(_take)/select_n | solution.py:93
  250.4 4.6 %copy.26 = bf16[256,8,768]{0,2,1:T(8,128)(2,1)} copy(bf16[256,8,768]{2,0,1:T(8,128)(2,1)} %select_bitcast_fusion) | data formatting | bytes 6291456 | tf_op jit(solution)/shard_map/jit(_take)/select_n | solution.py:93
  255.1 4.7 %copy.27 = bf16[256,6144]{1,0:T(8,128)(2,1)} copy(bf16[256,6144]{0,1:T(8,128)(2,1)} %bitcast.34) | data formatting | bytes 6291456
  (32 shorter events, 1.4 us)
Async XLA Ops:
  7.2 1.4 copy-start
  7.2 3.5 %copy-start.2 = (bf16[128,6144]{1,0:T(8,128)(2,1)S(1)}, bf16[128,6144]{1,0:T(8,128)(2,1)}, u32[]{:S(2)}) copy-start(bf16[128,6144]{1,0:T(8,128)(2,1)} %param.13) | copy-start | bytes 4718596
  7.2 225.7 %all-gather.3.cloned.1.call-start = ((), (), s32[]{:S(2)}) async-start(), calls=%async_computation.1 | async-start | bytes 3538944 | tf_op jit(solution)/shard_map/all_gather | solution.py:92
  8.6 2.1 copy-start.3
  11.9 38.1 %collective-permute-start = (bf16[128,6144]{1,0:T(8,128)(2,1)S(1)}, bf16[128,6144]{1,0:T(8,128)(2,1)S(1)}, u32[]{:S(2)}, u32[]{:S(2)}) collective-permute-start(bf16[128,6144]{1,0:T(8,128)(2,1)S(1)} %fusion), channel_id=1, source_target_pairs={{8,0},{16,8},{24,16},{9,1},{17,9},{25,17},{10,2},{18,10},{26,18},{... | collective-permute-start | bytes 4718600 | tf_op jit(solution)/shard_map/ppermute | solution.py:12
  50.0 1.2 copy-start.4
  51.2 36.5 %collective-permute-start.1 = (bf16[128,6144]{1,0:T(8,128)(2,1)S(1)}, bf16[128,6144]{1,0:T(8,128)(2,1)S(1)}, u32[]{:S(2)}, u32[]{:S(2)}) collective-permute-start(bf16[128,6144]{1,0:T(8,128)(2,1)S(1)} %add_convert_fusion.1), channel_id=1, source_target_pairs={{8,0},{16,8},{24,16},{9,1},{17,9},{25,17},{10,2},{18,10},{26,18},{... | collective-permute-start | bytes 4718600 | tf_op jit(solution)/shard_map/ppermute | solution.py:12
  87.7 2.3 copy-start.5
  88.3 3.1 %copy-start.8 = (s32[8]{0:T(128)S(1)}, s32[8]{0:T(128)}, u32[]{:S(2)}) copy-start(s32[8]{0:T(128)} %param.17) | copy-start | bytes 100
  90.1 35.9 %collective-permute-start.2 = (bf16[128,6144]{1,0:T(8,128)(2,1)}, bf16[128,6144]{1,0:T(8,128)(2,1)}, u32[]{:S(2)}, u32[]{:S(2)}) collective-permute-start(bf16[128,6144]{1,0:T(8,128)(2,1)} %add_convert_fusion), channel_id=1, source_target_pairs={{8,0},{16,8},{24,16},{9,1},{17,9},{25,17},{10,2},{18,10},{26,18},{... | collective-permute-start | bytes 4718600 | tf_op jit(solution)/shard_map/ppermute | solution.py:12
  92.4 37.5 %copy-start.6 = (bf16[128,6144]{1,0:T(8,128)(2,1)S(1)}, bf16[128,6144]{1,0:T(8,128)(2,1)}, u32[]{:S(2)}) copy-start(bf16[128,6144]{1,0:T(8,128)(2,1)} %param.10) | copy-start | bytes 4718596
  197.3 1.1 copy-start.7
  255.1 4.8 %copy-start.1 = (bf16[128,6144]{1,0:T(8,128)(2,1)S(1)}, bf16[128,6144]{1,0:T(8,128)(2,1)}, u32[]{:S(2)}) copy-start(bf16[128,6144]{1,0:T(8,128)(2,1)} %param.12) | copy-start | bytes 4718596
Sparse Core Ops, SparseCore 0:
  201.2 31.6 all-gather.2
where the time goes:
time: 268 us; the launch traced here: 267 us
  waiting for transfers between devices  132 us (49%)
  blocking collectives  42.6 us (16%)
  local copies, waits for them, and re-layouts  29.4 us (11%)
  other arithmetic  28.3 us (11%)
  matrix products  15.6 us (6%)
  between operations  14.9 us (6%)
  starting transfers between devices  3.9 us (1%)
    ppermute x3, waiting for transfers between devices, passed_along(): return lax.ppermute(block, axis, route)  106 us
    all_to_all x1, blocking collectives, on_device(): lax.all_to_all(outgoing, 'dp', split_axis=1, concat_axis=1, tiled=True)  42.6 us
    all_gather x1, waiting for transfers between devices, on_device(): lax.all_gather(server_packed[:, None, :], 'dp', axis=1, tiled=True)  26.2 us
    all_gather x2, local copies, waits for them, and re-layouts, on_device(): lax.all_gather(server_packed[:, None, :], 'dp', axis=1, tiled=True)  9.27 us
    reduce_sum x2, other arithmetic, on_device(): jnp.mean(jnp.abs(blocks), axis=(0, 2), keepdims=True) + epsilon  7.37 us
    unnamed x19, local copies, waits for them, and re-layouts  6.83 us
    convert_element_type x1, other arithmetic, on_device(): packed = (group_scale * jnp.tanh(blocks / group_scale)).astype(jnp.bfloat16)  5.81 us
    convert_element_type x1, other arithmetic, on_device(): new_worker = (blocks - packed.astype(jnp.float32)).astype(jnp.bfloat16).r...  5.57 us
  transfers between devices with their start and end apart: 4, of which 4 were waited for; matrix products, arithmetic and copies ran while one was open for 2% of the time, Pallas kernels for 0%

commit v1 on v0

--- a/solution.py
+++ b/solution.py
@@ -1,6 +1,10 @@
+import functools
+
 import jax
 import jax.numpy as jnp
 from jax import lax
+from jax.experimental import pallas as pl
+from jax.experimental.pallas import tpu as pltpu
 from jax.sharding import PartitionSpec as P
 
 epsilon = 1e-06
@@ -94,6 +98,486 @@
     return (new_momentum, new_worker, new_server)
 
 
+MESH = pl.DeviceIdType.MESH
+slope_c = 0.7978845608028654
+slope_k = 0.044715
+row_step = 32
+
+
+def fused_kernel(
+    group_ref,
+    x_hbm,
+    g_hbm,
+    u_hbm,
+    v_hbm,
+    m_hbm,
+    e_hbm,
+    se_hbm,
+    mom_out,
+    work_out,
+    serv_out,
+    x_v,
+    g_v,
+    u_v,
+    v_v,
+    m_v,
+    e_v,
+    se_v,
+    ups,
+    pres,
+    act_t,
+    slope_v,
+    pre_v,
+    pre_t,
+    dact,
+    comb,
+    own_pack,
+    own_sum,
+    work_v,
+    sib_out,
+    sib_in,
+    rs_out,
+    rs_in,
+    gath,
+    in_sem,
+    out_sem,
+    z_send,
+    z_recv,
+    up_send,
+    up_recv,
+    pre_send,
+    pre_recv,
+    sib_send,
+    sib_recv,
+    rs_send,
+    rs_recv,
+    ag_send,
+    ag_recv,
+):
+    sec = lax.axis_index("pipe")
+    me = lax.axis_index("dp")
+    sections = lax.axis_size("pipe")
+    ranks = lax.axis_size("dp")
+    toks, width = x_hbm.shape
+    units = u_v.shape[0]
+    group_cols = width // ranks
+    piece = units // ranks
+    core = me % 2
+    x_bit = (me // 2) % 2
+    y_bit = me // 4
+    sib = me + 1 - 2 * core
+    nbr_x = me + 2 - 4 * x_bit
+    nbr_y = me + 4 - 8 * y_bit
+    diag = nbr_x + 4 - 8 * y_bit
+    flip = 1 - 2 * core
+    peers = (nbr_x, nbr_y, diag)
+
+    def remote(src, dst, send, recv, pipe, dp):
+        return pltpu.make_async_remote_copy(
+            src_ref=src,
+            dst_ref=dst,
+            send_sem=send,
+            recv_sem=recv,
+            device_id=(pipe, dp),
+            device_id_type=MESH,
+        )
+
+    def whole(src, dst, i):
+        return [pltpu.make_async_copy(src, dst, in_sem.at[i, 0])]
+
+    def grouped(src, dst, i):
+        return [
+            pltpu.make_async_copy(
+                src.at[:, pl.ds(c * group_cols, group_cols)], dst.at[c], in_sem.at[i, c]
+            )
+            for c in range(ranks)
+        ]
+
+    loads = [
+        whole(u_hbm, u_v, 0),
+        grouped(x_hbm, x_v, 1),
+        whole(v_hbm, v_v, 2),
+        grouped(g_hbm, g_v, 3),
+        grouped(m_hbm, m_v, 4),
+        grouped(e_hbm, e_v, 5),
+        whole(se_hbm, se_v, 6),
+    ]
+    for copies in loads:
+        for load in copies:
+            load.start()
+
+    def loaded(i):
+        for load in loads[i]:
+            load.wait()
+
+    barrier = pltpu.get_barrier_semaphore()
+    for peer in (sib,) + peers:
+        pl.semaphore_signal(barrier, inc=1, device_id=(sec, peer), device_id_type=MESH)
+    for hop in range(1, sections):
+        pl.semaphore_signal(
+            barrier, inc=1, device_id=((sec + hop) % sections, me), device_id_type=MESH
+        )
+    pl.semaphore_wait(barrier, 3 + sections)
+
+    def up_rows(j, rank):
+        return ups.at[j - 1, pl.ds(pl.multiple_of(rank * piece, piece), piece)]
+
+    def own_rows():
+        return u_hbm.at[pl.ds(pl.multiple_of(me * piece, piece), piece)]
+
+    def send_up(target):
+        dst = ups.at[
+            jnp.maximum(sec - 1, 0), pl.ds(pl.multiple_of(me * piece, piece), piece)
+        ]
+        return remote(own_rows(), dst, z_send.at[target], z_recv.at[jnp.maximum(sec - 1, 0)], target, me)
+
+    for target in range(sections - 1):
+
+        @pl.when(target < sec)
+        def _():
+            send_up(target).start()
+
+    def spread_copy(place, send, recv, i):
+        if i < 3:
+            return remote(place(me), place(me), send.at[i], recv.at[i], sec, peers[i])
+        source = me if i == 3 else peers[i - 4]
+        return remote(place(source), place(source), send.at[i], recv.at[i], sec, sib)
+
+    def arrive(place, send, recv, i):
+        source = peers[i] if i < 3 else (me if i == 3 else peers[i - 4]) + flip
+        remote(place(source), place(source), send.at[i], recv.at[i], sec, sib).wait_recv()
+
+    def spread_start(place, send, recv):
+        for i in (2, 0, 1, 3):
+            spread_copy(place, send, recv, i).start()
+
+    def spread_relay(place, send, recv):
+        for i in (0, 1, 2):
+            arrive(place, send, recv, i)
+            spread_copy(place, send, recv, 4 + i).start()
+
+    def spread_finish(place, send, recv):
+        for i in (3, 4, 5, 6):
+            arrive(place, send, recv, i)
+
+    def spread_drain(place, send, recv):
+        for i in range(7):
+            spread_copy(place, send, recv, i).wait_send()
+
+    def up_args(j):
+        return (lambda rank: up_rows(j, rank), up_send.at[j - 1], up_recv.at[j - 1])
+
+    contract = (((1,), (1,)), ((), ()))
+    chunks = ranks
+
+    def cols_of(i):
+        return pl.ds(pl.multiple_of(i * group_cols, group_cols), group_cols)
+
+    def contracted(left, right):
+        dact[...] = jnp.zeros_like(dact)
+
+        @pl.loop(0, chunks)
+        def _(i):
+            dact[...] += lax.dot_general(
+                left[i],
+                right[:, cols_of(i)],
+                contract,
+                preferred_element_type=jnp.float32,
+            )
+
+    loaded(0)
+    loaded(1)
+    contracted(x_v, u_v)
+    pre = dact[...]
+    tanh = jnp.tanh(slope_c * (pre + slope_k * (pre * pre * pre)))
+    act = 0.5 * pre * (1.0 + tanh)
+    act_t[...] = jnp.transpose(act).astype(jnp.bfloat16)
+    slope_v[...] = 0.5 * (1.0 + tanh) + (0.5 * slope_c) * pre * (1.0 - tanh * tanh) * (
+        1.0 + 3.0 * slope_k * (pre * pre)
+    )
+    loaded(2)
+    loaded(3)
+
+    for j in range(1, sections):
+
+        @pl.when(j > sec)
+        def _():
+            remote(
+                up_rows(j, me), up_rows(j, me), z_send.at[0], z_recv.at[j - 1], sec, sib
+            ).wait_recv()
+            spread_start(*up_args(j))
+
+    for j in range(1, sections):
+
+        @pl.when(j > sec)
+        def _():
+            spread_relay(*up_args(j))
+
+    for j in range(sections - 1, 0, -1):
+
+        @pl.when(j > sec)
+        def _():
+            spread_finish(*up_args(j))
+            remote(
+                pres.at[j - 1], pres.at[j - 1], pre_send.at[0], pre_recv.at[j - 1], sec, sib
+            ).wait_recv()
+
+            @pl.loop(0, chunks)
+            def _(i):
+                step = jnp.dot(
+                    pres[j - 1], ups[j - 1, :, cols_of(i)], preferred_element_type=jnp.float32
+                )
+                g_v[i] = (g_v[i].astype(jnp.float32) + step).astype(jnp.bfloat16)
+
+    contracted(g_v, v_v)
+    d_pre = dact[...] * slope_v[...]
+    pre_v[...] = d_pre.astype(jnp.bfloat16)
+    pre_t[...] = jnp.transpose(d_pre).astype(jnp.bfloat16)
+
+    def send_pre(target):
+        slot = jnp.maximum(sec - 1, 0)
+        return remote(pre_v, pres.at[slot], pre_send.at[target], pre_recv.at[slot], target, me)
+
+    for target in range(sections - 2, -1, -1):
+
+        @pl.when(target < sec)
+        def _():
+            send_pre(target).start()
+
+    for i in (4, 5, 6):
+        loaded(i)
+
+    rows = m_hbm.shape[0]
+    entries = rows * group_cols
+    steps = rows // row_step
+
+    def rows_of(i):
+        return pl.ds(pl.multiple_of(i * row_step, row_step), row_step)
+
+    def magnitude(ref):
+        def body(i, total):
+            return total + jnp.abs(ref[rows_of(i)])
+
+        total = lax.fori_loop(0, steps, body, jnp.zeros((row_step, group_cols), jnp.float32))
+        return jnp.sum(total) / entries + epsilon
+
+    def pack(rank, into):
+        group = group_ref[rank]
+        for half, (weights, values) in enumerate(((pre_t, x_v), (act_t, g_v))):
+            part = pl.ds(half * units, units)
+            comb[part] = (
+                0.9 * m_v[group, part].astype(jnp.float32)
+                + 0.1 * jnp.dot(weights[...], values[group], preferred_element_type=jnp.float32)
+                + e_v[group, part].astype(jnp.float32)
+            )
+        scale = magnitude(comb)
+
+        @pl.loop(0, steps)
+        def _(i):
+            value = comb[rows_of(i)]
+            packed = (scale * jnp.tanh(value / scale)).astype(jnp.bfloat16)
+            into[rows_of(i)] = packed
+            work_v[rank, rows_of(i)] = (value - packed.astype(jnp.float32)).astype(jnp.bfloat16)
+
+        pltpu.make_async_copy(work_v.at[rank], work_out.at[rank], out_sem.at[rank]).start()
+
+    dests = (diag, nbr_x, nbr_y, me)
+
+    def sib_copy(i):
+        return remote(sib_out.at[i], sib_in.at[i], sib_send.at[i], sib_recv.at[i], sec, sib)
+
+    def rs_copy(i):
+        return remote(rs_out.at[i], rs_in.at[i], rs_send.at[i], rs_recv.at[i], sec, dests[i])
+
+    for i, dest in enumerate(dests):
+        pack(dest + flip, sib_out.at[i])
+        sib_copy(i).start()
+        pack(dest, own_pack)
+        sib_copy(i).wait_recv()
+
+        @pl.loop(0, steps)
+        def _(k):
+            both = own_pack[rows_of(k)].astype(jnp.float32) + sib_in[i, rows_of(k)].astype(
+                jnp.float32
+            )
+            if i < 3:
+                rs_out[i, rows_of(k)] = both.astype(jnp.bfloat16)
+            else:
+                own_sum[rows_of(k)] = both
+
+        if i < 3:
+            rs_copy(i).start()
+
+    for i in range(3):
+        rs_copy(i).wait_recv()
+
+    @pl.loop(0, steps)
+    def _(k):
+        total = own_sum[rows_of(k)]
+        for i in range(3):
+            total = total + rs_in[i, rows_of(k)].astype(jnp.float32)
+        comb[rows_of(k)] = total / ranks + se_v[rows_of(k)]
+
+    scale = magnitude(comb)
+
+    @pl.loop(0, steps)
+    def _(k):
+        value = comb[rows_of(k)]
+        packed = (scale * jnp.tanh(value / scale)).astype(jnp.bfloat16)
+        gath[me, rows_of(k)] = packed
+        own_sum[rows_of(k)] = value - packed.astype(jnp.float32)
+
+    def gath_args():
+        return (lambda rank: gath.at[rank], ag_send, ag_recv)
+
+    spread_start(*gath_args())
+    serv_copy = pltpu.make_async_copy(own_sum, serv_out, in_sem.at[0, 0])
+    serv_copy.start()
+
+    for rank in range(ranks):
+        pltpu.make_async_copy(work_v.at[rank], work_out.at[rank], out_sem.at[rank]).wait()
+    spread_relay(*gath_args())
+    spread_finish(*gath_args())
+    serv_copy.wait()
+    mom_copy = pltpu.make_async_copy(gath, mom_out, in_sem.at[1, 0])
+    mom_copy.start()
+    spread_drain(*gath_args())
+    for i in range(4):
+        sib_copy(i).wait_send()
+    for i in range(3):
+        rs_copy(i).wait_send()
+    for target in range(sections - 1):
+
+        @pl.when(target < sec)
+        def _():
+            send_up(target).wait_send()
+            send_pre(target).wait_send()
+
+    for j in range(1, sections):
+
+        @pl.when(j > sec)
+        def _():
+            spread_drain(*up_args(j))
+
+    mom_copy.wait()
+
+
+def place_kernel(owner_ref, mom_ref, work_ref, serv_ref, mom_out, work_out, serv_out):
+    mom_out[...] = mom_ref[0]
+    work_out[...] = work_ref[0]
+    serv_out[...] = serv_ref[...]
+
+
+def fused_on_device(
+    section_inputs,
+    out_grad,
+    up_weight,
+    down_weight,
+    momentum,
+    worker_error,
+    server_error,
+    owner_map,
+):
+    sections = lax.axis_size("pipe")
+    ranks = lax.axis_size("dp")
+    toks, width = section_inputs.shape
+    units = up_weight.shape[0]
+    rows = momentum.shape[0]
+    group_cols = width // ranks
+    bf16, f32 = jnp.bfloat16, jnp.float32
+    dma = pltpu.SemaphoreType.DMA
+    hbm = pl.BlockSpec(memory_space=pl.ANY)
+    block = (rows, group_cols)
+    order = jnp.arange(ranks, dtype=jnp.int32)
+    rank_group = jnp.sum(jnp.where(owner_map[None, :] == order[:, None], order[None, :], 0), axis=1)
+    moms, works, serv = pl.pallas_call(
+        fused_kernel,
+        out_shape=(
+            jax.ShapeDtypeStruct((ranks,) + block, bf16),
+            jax.ShapeDtypeStruct((ranks,) + block, bf16),
+            jax.ShapeDtypeStruct(block, f32),
+        ),
+        in_specs=[pl.BlockSpec(memory_space=pltpu.SMEM)] + [hbm] * 7,
+        out_specs=(hbm, hbm, hbm),
+        scratch_shapes=[
+            pltpu.VMEM((ranks, toks, group_cols), bf16),
+            pltpu.VMEM((ranks, toks, group_cols), bf16),
+            pltpu.VMEM((units, width), bf16),
+            pltpu.VMEM((units, width), bf16),
+            pltpu.VMEM((ranks,) + block, bf16),
+            pltpu.VMEM((ranks,) + block, bf16),
+            pltpu.VMEM(block, f32),
+            pltpu.VMEM((sections - 1, units, width), bf16),
+            pltpu.VMEM((sections - 1, toks, units), bf16),
+            pltpu.VMEM((units, toks), bf16),
+            pltpu.VMEM((toks, units), f32),
+            pltpu.VMEM((toks, units), bf16),
+            pltpu.VMEM((units, toks), bf16),
+            pltpu.VMEM((toks, units), f32),
+            pltpu.VMEM(block, f32),
+            pltpu.VMEM(block, bf16),
+            pltpu.VMEM(block, f32),
+            pltpu.VMEM((ranks,) + block, bf16),
+            pltpu.VMEM((4,) + block, bf16),
+            pltpu.VMEM((4,) + block, bf16),
+            pltpu.VMEM((3,) + block, bf16),
+            pltpu.VMEM((3,) + block, bf16),
+            pltpu.VMEM((ranks,) + block, bf16),
+            dma((7, ranks)),
+            dma((ranks,)),
+            dma((sections - 1,)),
+            dma((sections - 1,)),
+            dma((sections - 1, 7)),
+            dma((sections - 1, 7)),
+            dma((sections - 1,)),
+            dma((sections - 1,)),
+            dma((4,)),
+            dma((4,)),
+            dma((3,)),
+            dma((3,)),
+            dma((7,)),
+            dma((7,)),
+        ],
+        compiler_params=pltpu.CompilerParams(
+            collective_id=0, has_side_effects=True, vmem_limit_bytes=56 * 1024 * 1024
+        ),
+        name="adapter_step",
+    )(
+        rank_group,
+        section_inputs,
+        out_grad,
+        up_weight,
+        down_weight,
+        momentum,
+        worker_error,
+        server_error,
+    )
+    part = rows // ranks
+    return pl.pallas_call(
+        place_kernel,
+        out_shape=(
+            jax.ShapeDtypeStruct((rows, width), bf16),
+            jax.ShapeDtypeStruct((rows, width), bf16),
+            jax.ShapeDtypeStruct(block, f32),
+        ),
+        grid_spec=pltpu.PrefetchScalarGridSpec(
+            num_scalar_prefetch=1,
+            grid=(ranks,),
+            in_specs=[
+                pl.BlockSpec((1,) + block, lambda c, owner: (owner[c], 0, 0)),
+                pl.BlockSpec((1,) + block, lambda c, owner: (owner[c], 0, 0)),
+                pl.BlockSpec((part, group_cols), lambda c, owner: (c, 0)),
+            ],
+            out_specs=[
+                pl.BlockSpec(block, lambda c, owner: (0, c)),
+                pl.BlockSpec(block, lambda c, owner: (0, c)),
+                pl.BlockSpec((part, group_cols), lambda c, owner: (c, 0)),
+            ],
+        ),
+        name="place_groups",
+    )(owner_map, moms, works, serv)
+
+
 def solution(mesh):
     in_specs = (
         P(("pipe", "dp"), None),
@@ -106,6 +590,7 @@
         P(),
     )
     out_specs = (P("pipe", None), P("pipe", "dp"), P("pipe", "dp"))
+    fits = mesh.shape["dp"] == 8 and mesh.shape["pipe"] == 4
     return jax.shard_map(
-        on_device, mesh=mesh, in_specs=in_specs, out_specs=out_specs, check_vma=False
-    )
+        fused_on_device if fits else on_device, mesh=mesh, in_specs=in_specs, out_specs=out_specs, check_vma=False
+    )

time: 268 us -> 114 us (0.43)
  waiting for transfers between devices: 132 us -> 0 us
  Pallas kernels: 0 us -> 112 us
  blocking collectives: 42.6 us -> 0 us
  local copies, waits for them, and re-layouts: 29.4 us -> 0 us
  other arithmetic: 28.3 us -> 1.28 us
  matrix products: 15.6 us -> 0 us
  between operations: 14.9 us -> 0.64 us
  starting transfers between devices: 3.9 us -> 0 us
    pallas_call x0 -> x2, Pallas kernels: none -> 112 us  [the longest x1 103 us: fused_on_device(): pl.pallas_call(fused_kernel, out_shape=(jax.ShapeDtypeStruct((ranks,) + b...]
    ppermute x3 -> x0, waiting for transfers between devices: 106 us -> none  [passed_along(): return lax.ppermute(block, axis, route)]
    all_to_all x1 -> x0, blocking collectives: 42.6 us -> none  [on_device(): lax.all_to_all(outgoing, 'dp', split_axis=1, concat_axis=1, tiled=True)]
    all_gather x1 -> x0, waiting for transfers between devices: 26.2 us -> none  [on_device(): lax.all_gather(server_packed[:, None, :], 'dp', axis=1, tiled=True)]
    dot_general x9 -> x0, matrix products: 15.6 us -> none  [the longest x1 5 us: on_device(): lax.dot_general(kept_pre, section_inputs, token_contract, preferred_eleme...]
    convert_element_type x2 -> x0, other arithmetic: 11.4 us -> none  [the longest x1 5.81 us: on_device(): packed = (group_scale * jnp.tanh(blocks / group_scale)).astype(jnp.bfloat16)]
    all_gather x2 -> x0, local copies, waits for them, and re-layouts: 9.27 us -> none  [on_device(): lax.all_gather(server_packed[:, None, :], 'dp', axis=1, tiled=True)]
    gather x2 -> x0, local copies, waits for them, and re-layouts: 8.6 us -> none  [the longest x1 4.3 us: on_device(): outgoing = jnp.take(packed, rank_group, axis=1)]
  transfers between devices with their start and end apart: 4 -> 0, of which waited for: 4 -> 0; matrix products, arithmetic and copies ran while one was open for 2% -> 0% of each run, Pallas kernels for 0% -> 0%
where the time goes in v1:
time: 114 us
  Pallas kernels  112 us (98%)
  other arithmetic  1.28 us (1%)
    pallas_call x1, Pallas kernels, fused_on_device(): pl.pallas_call(fused_kernel, out_shape=(jax.ShapeDtypeStruct((ranks,) + b...  103 us
    pallas_call x1, Pallas kernels, fused_on_device(): pl.pallas_call(place_kernel, out_shape=(jax.ShapeDtypeStruct((rows, width...  8.74 us

profile of v1, /device:TPU:1, one launch (start us, length us, event | category | flops | bytes accessed | tf_op | source)
XLA Modules:
  0.0 113.8 jit_solution(5588454439442102272)
XLA Ops:
  0.6 1.3 %select_reduce_fusion.group_ref = s32[8]{0:T(128)} fusion(s32[8]{0:T(128)} %owner_ref.1), kind=kLoop, calls=%fused_computation | loop fusion | flops 184 | bytes 64 | tf_op jit(solution)/shard_map/reduce_sum | solution.py:492
  1.9 103.2 %adapter_step.1 = (bf16[8,256,768]{2,1,0:T(8,128)(2,1)}, bf16[8,256,768]{2,1,0:T(8,128)(2,1)}, f32[256,768]{1,0:T(8,128)}) custom-call(s32[8]{0:T(128)} %select_reduce_fusion.group_ref, bf16[128,6144]{1,0:T(8,128)(2,1)} %x_hbm.1, bf16[128,6144]{1,0:T(8,128)(2,1)} %g_hbm.1, bf16[128,6144]{1,0:T(8,128)(2,1)} %u_hbm.1, bf16[128,6144]{1,0:T(8,128)(2,1)} %v_hbm.1, ...), custom_call_target="tpu_custom_call" | custom-call | tf_op jit(solution)/shard_map/adapter_step/pallas_call | solution.py:493
  105.1 8.7 %place_groups.1 = (bf16[256,6144]{1,0:T(8,128)(2,1)}, bf16[256,6144]{1,0:T(8,128)(2,1)}, f32[256,768]{1,0:T(8,128)}) custom-call(s32[8]{0:T(128)} %owner_ref.1, bf16[8,256,768]{2,1,0:T(8,128)(2,1)} %get-tuple-element.6.mom_ref, bf16[8,256,768]{2,1,0:T(8,128)(2,1)} %get-tuple-element.7.work_ref, f32[256,768]{1,0:T(8,128)} %get-tuple-element.8.serv_ref), custom_call_target="tpu_custom_call" | custom-call | tf_op jit(solution)/shard_map/place_groups/pallas_call | solution.py:556

commit v2 on v1

--- a/solution.py
+++ b/solution.py
@@ -102,6 +102,7 @@
 slope_c = 0.7978845608028654
 slope_k = 0.044715
 row_step = 32
+col_step = 256
 
 
 def fused_kernel(
@@ -219,53 +220,83 @@
         )
     pl.semaphore_wait(barrier, 3 + sections)
 
-    def up_rows(j, rank):
-        return ups.at[j - 1, pl.ds(pl.multiple_of(rank * piece, piece), piece)]
-
-    def own_rows():
-        return u_hbm.at[pl.ds(pl.multiple_of(me * piece, piece), piece)]
-
-    def send_up(target):
-        dst = ups.at[
-            jnp.maximum(sec - 1, 0), pl.ds(pl.multiple_of(me * piece, piece), piece)
-        ]
-        return remote(own_rows(), dst, z_send.at[target], z_recv.at[jnp.maximum(sec - 1, 0)], target, me)
-
-    for target in range(sections - 1):
-
-        @pl.when(target < sec)
+    def up_rows(j, rank, part=None):
+        rows = pl.ds(pl.multiple_of(rank * piece, piece), piece)
+        if part is None:
+            return ups.at[j - 1, rows]
+        return ups.at[j - 1, rows, pl.ds(part * (width // 2), width // 2)]
+
+    def z_own(j):
+        rows = pl.ds(pl.multiple_of(me * piece, piece), piece)
+        return remote(u_hbm.at[rows], up_rows(j, me), z_send.at[j - 1], z_recv.at[j - 1], j - 1, me)
+
+    def z_pass(j):
+        return remote(
+            up_rows(j, me),
+            up_rows(j, me),
+            z_send.at[j - 1],
+            z_recv.at[j - 1],
+            jnp.maximum(sec - 1, 0),
+            me,
+        )
+
+    for j in range(1, sections):
+
+        @pl.when(sec == j)
         def _():
-            send_up(target).start()
+            z_own(j).start()
 
     def spread_copy(place, send, recv, i):
-        if i < 3:
-            return remote(place(me), place(me), send.at[i], recv.at[i], sec, peers[i])
-        source = me if i == 3 else peers[i - 4]
-        return remote(place(source), place(source), send.at[i], recv.at[i], sec, sib)
+        ref, peer = (
+            (place(me), nbr_x),
+            (place(me), nbr_y),
+            (place(nbr_x, 0), nbr_y),
+            (place(nbr_y, 1), nbr_x),
+            (place(me), sib),
+            (place(nbr_x), sib),
+            (place(nbr_y), sib),
+            (place(diag), sib),
+        )[i]
+        return remote(ref, ref, send.at[i], recv.at[i], sec, peer)
 
     def arrive(place, send, recv, i):
-        source = peers[i] if i < 3 else (me if i == 3 else peers[i - 4]) + flip
-        remote(place(source), place(source), send.at[i], recv.at[i], sec, sib).wait_recv()
-
-    def spread_start(place, send, recv):
-        for i in (2, 0, 1, 3):
-            spread_copy(place, send, recv, i).start()
-
-    def spread_relay(place, send, recv):
-        for i in (0, 1, 2):
-            arrive(place, send, recv, i)
-            spread_copy(place, send, recv, 4 + i).start()
-
-    def spread_finish(place, send, recv):
-        for i in (3, 4, 5, 6):
-            arrive(place, send, recv, i)
-
-    def spread_drain(place, send, recv):
-        for i in range(7):
-            spread_copy(place, send, recv, i).wait_send()
+        ref = (
+            place(nbr_x),
+            place(nbr_y),
+            place(diag, 0),
+            place(diag, 1),
+            place(sib),
+            place(nbr_x + flip),
+            place(nbr_y + flip),
+            place(diag + flip),
+        )[i]
+        remote(ref, ref, send.at[i], recv.at[i], sec, sib).wait_recv()
+
+    def spread_start(*where):
+        for i in (0, 1, 4):
+            spread_copy(*where, i).start()
+
+    def spread_pass(*where):
+        for i in (0, 1):
+            arrive(*where, i)
+            spread_copy(*where, 2 + i).start()
+            spread_copy(*where, 5 + i).start()
+
+    def spread_diag(*where):
+        arrive(*where, 2)
+        arrive(*where, 3)
+        spread_copy(*where, 7).start()
+
+    def spread_finish(*where):
+        for i in (4, 5, 6, 7):
+            arrive(*where, i)
+
+    def spread_drain(*where):
+        for i in range(8):
+            spread_copy(*where, i).wait_send()
 
     def up_args(j):
-        return (lambda rank: up_rows(j, rank), up_send.at[j - 1], up_recv.at[j - 1])
+        return (functools.partial(up_rows, j), up_send.at[j - 1], up_recv.at[j - 1])
 
     contract = (((1,), (1,)), ((), ()))
     chunks = ranks
@@ -298,20 +329,28 @@
     loaded(2)
     loaded(3)
 
-    for j in range(1, sections):
-
-        @pl.when(j > sec)
+    def z_step(j):
+        z_pass(j).wait_recv()
+
+        @pl.when(sec > 0)
         def _():
-            remote(
-                up_rows(j, me), up_rows(j, me), z_send.at[0], z_recv.at[j - 1], sec, sib
-            ).wait_recv()
-            spread_start(*up_args(j))
-
-    for j in range(1, sections):
-
-        @pl.when(j > sec)
-        def _():
-            spread_relay(*up_args(j))
+            z_pass(j).start()
+
+        spread_start(*up_args(j))
+
+    turns = []
+    for turn in range(1, sections + 3):
+        for lag, step in ((3, spread_diag), (2, spread_pass), (0, z_step)):
+            turns.append((step, turn - lag))
+    for step, j in turns:
+        if 1 <= j < sections:
+
+            @pl.when(j > sec)
+            def _():
+                if step is z_step:
+                    z_step(j)
+                else:
+                    step(*up_args(j))
 
     for j in range(sections - 1, 0, -1):
 
@@ -363,19 +402,30 @@
 
     def pack(rank, into):
         group = group_ref[rank]
+        total = jnp.zeros((8, col_step), jnp.float32)
         for half, (weights, values) in enumerate(((pre_t, x_v), (act_t, g_v))):
             part = pl.ds(half * units, units)
-            comb[part] = (
-                0.9 * m_v[group, part].astype(jnp.float32)
-                + 0.1 * jnp.dot(weights[...], values[group], preferred_element_type=jnp.float32)
-                + e_v[group, part].astype(jnp.float32)
-            )
-        scale = magnitude(comb)
+            for k in range(group_cols // col_step):
+                cols = pl.ds(k * col_step, col_step)
+                value = (
+                    0.9 * m_v[group, part, cols].astype(jnp.float32)
+                    + 0.1
+                    * jnp.dot(
+                        weights[...], values[group, :, cols], preferred_element_type=jnp.float32
+                    )
+                    + e_v[group, part, cols].astype(jnp.float32)
+                )
+                comb[part, cols] = value
+                total = total + jnp.sum(
+                    jnp.abs(value).reshape(units // 8, 8, col_step), axis=0
+                )
+        scale = jnp.sum(total) / entries + epsilon
+        inverse = 1.0 / scale
 
         @pl.loop(0, steps)
         def _(i):
             value = comb[rows_of(i)]
-            packed = (scale * jnp.tanh(value / scale)).astype(jnp.bfloat16)
+            packed = (scale * jnp.tanh(value * inverse)).astype(jnp.bfloat16)
             into[rows_of(i)] = packed
             work_v[rank, rows_of(i)] = (value - packed.astype(jnp.float32)).astype(jnp.bfloat16)
 
@@ -419,29 +469,34 @@
         comb[rows_of(k)] = total / ranks + se_v[rows_of(k)]
 
     scale = magnitude(comb)
+    inverse = 1.0 / scale
 
     @pl.loop(0, steps)
     def _(k):
         value = comb[rows_of(k)]
-        packed = (scale * jnp.tanh(value / scale)).astype(jnp.bfloat16)
+        packed = (scale * jnp.tanh(value * inverse)).astype(jnp.bfloat16)
         gath[me, rows_of(k)] = packed
         own_sum[rows_of(k)] = value - packed.astype(jnp.float32)
 
-    def gath_args():
-        return (lambda rank: gath.at[rank], ag_send, ag_recv)
-
-    spread_start(*gath_args())
+    def gath_place(rank, part=None):
+        if part is None:
+            return gath.at[rank]
+        return gath.at[rank, pl.ds(part * (rows // 2), rows // 2)]
+
+    gath_args = (gath_place, ag_send, ag_recv)
+    spread_start(*gath_args)
     serv_copy = pltpu.make_async_copy(own_sum, serv_out, in_sem.at[0, 0])
     serv_copy.start()
 
     for rank in range(ranks):
         pltpu.make_async_copy(work_v.at[rank], work_out.at[rank], out_sem.at[rank]).wait()
-    spread_relay(*gath_args())
-    spread_finish(*gath_args())
+    spread_pass(*gath_args)
+    spread_diag(*gath_args)
+    spread_finish(*gath_args)
     serv_copy.wait()
     mom_copy = pltpu.make_async_copy(gath, mom_out, in_sem.at[1, 0])
     mom_copy.start()
-    spread_drain(*gath_args())
+    spread_drain(*gath_args)
     for i in range(4):
         sib_copy(i).wait_send()
     for i in range(3):
@@ -450,22 +505,38 @@
 
         @pl.when(target < sec)
         def _():
-            send_up(target).wait_send()
             send_pre(target).wait_send()
 
     for j in range(1, sections):
+
+        @pl.when(sec == j)
+        def _():
+            z_own(j).wait_send()
 
         @pl.when(j > sec)
         def _():
             spread_drain(*up_args(j))
 
+            @pl.when(sec > 0)
+            def _():
+                z_pass(j).wait_send()
+
     mom_copy.wait()
 
 
-def place_kernel(owner_ref, mom_ref, work_ref, serv_ref, mom_out, work_out, serv_out):
-    mom_out[...] = mom_ref[0]
-    work_out[...] = work_ref[0]
-    serv_out[...] = serv_ref[...]
+def place_kernel(owner_ref, mom_ref, work_ref, serv_ref, mom_out, work_out, serv_out, sem):
+    ranks, rows, cols = mom_ref.shape
+    copies = [pltpu.make_async_copy(serv_ref, serv_out, sem.at[2, 0])]
+    for c in range(ranks):
+        place = pl.ds(c * cols, cols)
+        for i, (src, dst) in enumerate(((mom_ref, mom_out), (work_ref, work_out))):
+            copies.append(
+                pltpu.make_async_copy(src.at[owner_ref[c]], dst.at[:, place], sem.at[i, c])
+            )
+    for copy in copies:
+        copy.start()
+    for copy in copies:
+        copy.wait()
 
 
 def fused_on_device(
@@ -527,16 +598,16 @@
             dma((ranks,)),
             dma((sections - 1,)),
             dma((sections - 1,)),
-            dma((sections - 1, 7)),
-            dma((sections - 1, 7)),
+            dma((sections - 1, 8)),
+            dma((sections - 1, 8)),
             dma((sections - 1,)),
             dma((sections - 1,)),
             dma((4,)),
             dma((4,)),
             dma((3,)),
             dma((3,)),
-            dma((7,)),
-            dma((7,)),
+            dma((8,)),
+            dma((8,)),
         ],
         compiler_params=pltpu.CompilerParams(
             collective_id=0, has_side_effects=True, vmem_limit_bytes=56 * 1024 * 1024
@@ -552,7 +623,6 @@
         worker_error,
         server_error,
     )
-    part = rows // ranks
     return pl.pallas_call(
         place_kernel,
         out_shape=(
@@ -560,20 +630,9 @@
             jax.ShapeDtypeStruct((rows, width), bf16),
             jax.ShapeDtypeStruct(block, f32),
         ),
-        grid_spec=pltpu.PrefetchScalarGridSpec(
-            num_scalar_prefetch=1,
-            grid=(ranks,),
-            in_specs=[
-                pl.BlockSpec((1,) + block, lambda c, owner: (owner[c], 0, 0)),
-                pl.BlockSpec((1,) + block, lambda c, owner: (owner[c], 0, 0)),
-                pl.BlockSpec((part, group_cols), lambda c, owner: (c, 0)),
-            ],
-            out_specs=[
-                pl.BlockSpec(block, lambda c, owner: (0, c)),
-                pl.BlockSpec(block, lambda c, owner: (0, c)),
-                pl.BlockSpec((part, group_cols), lambda c, owner: (c, 0)),
-            ],
-        ),
+        in_specs=[pl.BlockSpec(memory_space=pltpu.SMEM), hbm, hbm, hbm],
+        out_specs=(hbm, hbm, hbm),
+        scratch_shapes=[dma((3, ranks))],
         name="place_groups",
     )(owner_map, moms, works, serv)
 

time: 114 us -> 304 us (2.67)
  Pallas kernels: 112 us -> 302 us
    pallas_call x1, Pallas kernels: 8.74 us -> 216 us  [fused_on_device(): pl.pallas_call(place_kernel, out_shape=(jax.ShapeDtypeStruct((rows, width...]
    pallas_call x1, Pallas kernels: 103 us -> 85.4 us  [fused_on_device(): pl.pallas_call(fused_kernel, out_shape=(jax.ShapeDtypeStruct((ranks,) + b...]
where the time goes in v2:
time: 304 us
  Pallas kernels  302 us (99%)
    pallas_call x1, Pallas kernels, fused_on_device(): pl.pallas_call(place_kernel, out_shape=(jax.ShapeDtypeStruct((rows, width...  216 us
    pallas_call x1, Pallas kernels, fused_on_device(): pl.pallas_call(fused_kernel, out_shape=(jax.ShapeDtypeStruct((ranks,) + b...  85.4 us

profile of v2, /device:TPU:1, one launch (start us, length us, event | category | flops | bytes accessed | tf_op | source)
XLA Modules:
  0.0 303.7 jit_solution(16055997117012062071)
XLA Ops:
  0.6 1.3 select_reduce_fusion.group_ref
  1.9 85.4 %adapter_step.1 = (bf16[8,256,768]{2,1,0:T(8,128)(2,1)}, bf16[8,256,768]{2,1,0:T(8,128)(2,1)}, f32[256,768]{1,0:T(8,128)}) custom-call(s32[8]{0:T(128)} %select_reduce_fusion.group_ref, bf16[128,6144]{1,0:T(8,128)(2,1)} %x_hbm.1, bf16[128,6144]{1,0:T(8,128)(2,1)} %g_hbm.1, bf16[128,6144]{1,0:T(8,128)(2,1)} %u_hbm.1, bf16[128,6144]{1,0:T(8,128)(2,1)} %v_hbm.1, ...), custom_call_target="tpu_custom_call" | custom-call | tf_op jit(solution)/shard_map/adapter_step/pallas_call | solution.py:564
  87.3 216.4 %place_groups.1 = (bf16[256,6144]{1,0:T(8,128)(2,1)}, bf16[256,6144]{1,0:T(8,128)(2,1)}, f32[256,768]{1,0:T(8,128)}) custom-call(s32[8]{0:T(128)} %owner_ref.1, bf16[8,256,768]{2,1,0:T(8,128)(2,1)} %get-tuple-element.6.mom_ref, bf16[8,256,768]{2,1,0:T(8,128)(2,1)} %get-tuple-element.7.work_ref, f32[256,768]{1,0:T(8,128)} %get-tuple-element.8.serv_ref), custom_call_target="tpu_custom_call" | custom-call | tf_op jit(solution)/shard_map/place_groups/pallas_call | solution.py:626

commit v3 on v2

--- a/solution.py
+++ b/solution.py
@@ -103,6 +103,7 @@
 slope_k = 0.044715
 row_step = 32
 col_step = 256
+ag_chunks = 4
 
 
 def fused_kernel(
@@ -131,6 +132,7 @@
     pre_v,
     pre_t,
     dact,
+    mixed,
     comb,
     own_pack,
     own_sum,
@@ -305,70 +307,80 @@
         return pl.ds(pl.multiple_of(i * group_cols, group_cols), group_cols)
 
     def contracted(left, right):
-        dact[...] = jnp.zeros_like(dact)
-
-        @pl.loop(0, chunks)
-        def _(i):
-            dact[...] += lax.dot_general(
-                left[i],
+        total = jnp.zeros((toks, units), jnp.float32)
+        for i in range(chunks):
+            total = total + lax.dot_general(
+                left(i),
                 right[:, cols_of(i)],
                 contract,
                 preferred_element_type=jnp.float32,
             )
-
+        return total
+
+    def z_step(j):
+        z_pass(j).wait_recv()
+
+        @pl.when(sec > 0)
+        def _():
+            z_pass(j).start()
+
+        spread_start(*up_args(j))
+
+    above = sections - 1 - sec
+
+    def turn(step, k):
+        @pl.when(k <= above)
+        def _():
+            if step is z_step:
+                z_step(sec + k)
+            else:
+                step(*up_args(sec + k))
+
+    turn(z_step, 1)
     loaded(0)
     loaded(1)
-    contracted(x_v, u_v)
-    pre = dact[...]
+    pre = contracted(lambda i: x_v[i], u_v)
     tanh = jnp.tanh(slope_c * (pre + slope_k * (pre * pre * pre)))
     act = 0.5 * pre * (1.0 + tanh)
     act_t[...] = jnp.transpose(act).astype(jnp.bfloat16)
     slope_v[...] = 0.5 * (1.0 + tanh) + (0.5 * slope_c) * pre * (1.0 - tanh * tanh) * (
         1.0 + 3.0 * slope_k * (pre * pre)
     )
+    turn(z_step, 2)
     loaded(2)
     loaded(3)
-
-    def z_step(j):
-        z_pass(j).wait_recv()
-
-        @pl.when(sec > 0)
-        def _():
-            z_pass(j).start()
-
-        spread_start(*up_args(j))
-
-    turns = []
-    for turn in range(1, sections + 3):
-        for lag, step in ((3, spread_diag), (2, spread_pass), (0, z_step)):
-            turns.append((step, turn - lag))
-    for step, j in turns:
-        if 1 <= j < sections:
-
-            @pl.when(j > sec)
-            def _():
-                if step is z_step:
-                    z_step(j)
-                else:
-                    step(*up_args(j))
-
-    for j in range(sections - 1, 0, -1):
-
-        @pl.when(j > sec)
-        def _():
-            spread_finish(*up_args(j))
+    dact[...] = contracted(lambda i: g_v[i], v_v)
+    turn(spread_pass, 1)
+    turn(z_step, 3)
+    turn(spread_diag, 1)
+    turn(spread_pass, 2)
+
+    def cross(k):
+        @pl.when(k <= above)
+        def _():
+            spread_finish(*up_args(sec + k))
+            slot = sec + k - 1
+            mixed[slot] = contracted(lambda i: ups[slot, :, cols_of(i)], v_v)
+
+    cross(1)
+    turn(spread_diag, 2)
+    turn(spread_pass, 3)
+    cross(2)
+    turn(spread_diag, 3)
+    cross(3)
+
+    for k in range(sections - 1, 0, -1):
+
+        @pl.when(k <= above)
+        def _():
+            slot = sec + k - 1
             remote(
-                pres.at[j - 1], pres.at[j - 1], pre_send.at[0], pre_recv.at[j - 1], sec, sib
+                pres.at[slot], pres.at[slot], pre_send.at[0], pre_recv.at[slot], sec, sib
             ).wait_recv()
-
-            @pl.loop(0, chunks)
-            def _(i):
-                step = jnp.dot(
-                    pres[j - 1], ups[j - 1, :, cols_of(i)], preferred_element_type=jnp.float32
-                )
-                g_v[i] = (g_v[i].astype(jnp.float32) + step).astype(jnp.bfloat16)
-
-    contracted(g_v, v_v)
+            dact[...] += jnp.dot(
+                pres[slot].astype(jnp.float32), mixed[slot], precision=lax.Precision.HIGHEST
+            )
+
     d_pre = dact[...] * slope_v[...]
     pre_v[...] = d_pre.astype(jnp.bfloat16)
     pre_t[...] = jnp.transpose(d_pre).astype(jnp.bfloat16)
@@ -382,6 +394,17 @@
         @pl.when(target < sec)
         def _():
             send_pre(target).start()
+
+    for low in range(sections - 1):
+
+        @pl.when(sec == low)
+        def _():
+            @pl.loop(0, chunks)
+            def _(i):
+                wide = jnp.concatenate([pres[k] for k in range(low, sections - 1)], axis=1)
+                tall = ups[low:, :, cols_of(i)].reshape((sections - 1 - low) * units, group_cols)
+                step = jnp.dot(wide, tall, preferred_element_type=jnp.float32)
+                g_v[i] = (g_v[i].astype(jnp.float32) + step).astype(jnp.bfloat16)
 
     for i in (4, 5, 6):
         loaded(i)
@@ -478,25 +501,42 @@
         gath[me, rows_of(k)] = packed
         own_sum[rows_of(k)] = value - packed.astype(jnp.float32)
 
-    def gath_place(rank, part=None):
+    def gath_place(t, rank, part=None):
+        size = rows // ag_chunks
         if part is None:
-            return gath.at[rank]
-        return gath.at[rank, pl.ds(part * (rows // 2), rows // 2)]
-
-    gath_args = (gath_place, ag_send, ag_recv)
-    spread_start(*gath_args)
+            return gath.at[rank, pl.ds(t * size, size)]
+        return gath.at[rank, pl.ds(t * size + part * (size // 2), size // 2)]
+
+    def ag_args(t):
+        return (functools.partial(gath_place, t), ag_send.at[t], ag_recv.at[t])
+
+    for t in range(ag_chunks):
+        spread_start(*ag_args(t))
+
+    def keep(i, rank):
+        return pltpu.make_async_copy(gath.at[rank], mom_out.at[rank], in_sem.at[1, i])
+
+    kept = (me, nbr_x, nbr_y, diag, sib, nbr_x + flip, nbr_y + flip, diag + flip)
+    keep(0, me).start()
     serv_copy = pltpu.make_async_copy(own_sum, serv_out, in_sem.at[0, 0])
     serv_copy.start()
 
     for rank in range(ranks):
         pltpu.make_async_copy(work_v.at[rank], work_out.at[rank], out_sem.at[rank]).wait()
-    spread_pass(*gath_args)
-    spread_diag(*gath_args)
-    spread_finish(*gath_args)
+    for t in range(ag_chunks + 1):
+        if t < ag_chunks:
+            spread_pass(*ag_args(t))
+        if t > 0:
+            spread_diag(*ag_args(t - 1))
+    for i in (1, 2, 3):
+        keep(i, kept[i]).start()
     serv_copy.wait()
-    mom_copy = pltpu.make_async_copy(gath, mom_out, in_sem.at[1, 0])
-    mom_copy.start()
-    spread_drain(*gath_args)
+    for i in (4, 5, 6, 7):
+        for t in range(ag_chunks):
+            arrive(*ag_args(t), i)
+        keep(i, kept[i]).start()
+    for t in range(ag_chunks):
+        spread_drain(*ag_args(t))
     for i in range(4):
         sib_copy(i).wait_send()
     for i in range(3):
@@ -521,22 +561,33 @@
             def _():
                 z_pass(j).wait_send()
 
-    mom_copy.wait()
-
-
-def place_kernel(owner_ref, mom_ref, work_ref, serv_ref, mom_out, work_out, serv_out, sem):
+    for i in range(8):
+        keep(i, kept[i]).wait()
+
+
+def place_kernel(
+    owner_ref, mom_ref, work_ref, serv_ref, mom_out, work_out, serv_out, held, kept, load_sem, store_sem
+):
     ranks, rows, cols = mom_ref.shape
-    copies = [pltpu.make_async_copy(serv_ref, serv_out, sem.at[2, 0])]
-    for c in range(ranks):
-        place = pl.ds(c * cols, cols)
-        for i, (src, dst) in enumerate(((mom_ref, mom_out), (work_ref, work_out))):
-            copies.append(
-                pltpu.make_async_copy(src.at[owner_ref[c]], dst.at[:, place], sem.at[i, c])
+    loads = [pltpu.make_async_copy(serv_ref, kept, load_sem.at[2, 0])]
+    stores = [pltpu.make_async_copy(kept, serv_out, store_sem.at[2, 0])]
+    for i, (src, dst) in enumerate(((work_ref, work_out), (mom_ref, mom_out))):
+        for c in range(ranks):
+            loads.append(
+                pltpu.make_async_copy(src.at[owner_ref[c]], held.at[i, c], load_sem.at[i, c])
             )
-    for copy in copies:
-        copy.start()
-    for copy in copies:
-        copy.wait()
+            stores.append(
+                pltpu.make_async_copy(
+                    held.at[i, c], dst.at[:, pl.ds(c * cols, cols)], store_sem.at[i, c]
+                )
+            )
+    for load in loads:
+        load.start()
+    for load, store in zip(loads, stores):
+        load.wait()
+        store.start()
+    for store in stores:
+        store.wait()
 
 
 def fused_on_device(
@@ -585,6 +636,7 @@
             pltpu.VMEM((toks, units), bf16),
             pltpu.VMEM((units, toks), bf16),
             pltpu.VMEM((toks, units), f32),
+            pltpu.VMEM((sections - 1, units, units), f32),
             pltpu.VMEM(block, f32),
             pltpu.VMEM(block, bf16),
             pltpu.VMEM(block, f32),
@@ -606,8 +658,8 @@
             dma((4,)),
             dma((3,)),
             dma((3,)),
-            dma((8,)),
-            dma((8,)),
+            dma((ag_chunks, 8)),
+            dma((ag_chunks, 8)),
         ],
         compiler_params=pltpu.CompilerParams(
             collective_id=0, has_side_effects=True, vmem_limit_bytes=56 * 1024 * 1024
@@ -632,7 +684,13 @@
         ),
         in_specs=[pl.BlockSpec(memory_space=pltpu.SMEM), hbm, hbm, hbm],
         out_specs=(hbm, hbm, hbm),
-        scratch_shapes=[dma((3, ranks))],
+        scratch_shapes=[
+            pltpu.VMEM((2, ranks) + block, bf16),
+            pltpu.VMEM(block, f32),
+            dma((3, ranks)),
+            dma((3, ranks)),
+        ],
+        compiler_params=pltpu.CompilerParams(vmem_limit_bytes=60 * 1024 * 1024),
         name="place_groups",
     )(owner_map, moms, works, serv)
 

time: 304 us -> 89.4 us (0.29)
  Pallas kernels: 302 us -> 87.4 us
    pallas_call x1, Pallas kernels: 216 us -> 6.78 us  [fused_on_device(): pl.pallas_call(place_kernel, out_shape=(jax.ShapeDtypeStruct((rows, width...]
    pallas_call x1, Pallas kernels: 85.4 us -> 80.6 us  [fused_on_device(): pl.pallas_call(fused_kernel, out_shape=(jax.ShapeDtypeStruct((ranks,) + b...]
where the time goes in v3:
time: 89.4 us; the launch traced here: 89.3 us
  Pallas kernels  87.4 us (98%)
  other arithmetic  1.28 us (1%)
    pallas_call x1, Pallas kernels, fused_on_device(): pl.pallas_call(fused_kernel, out_shape=(jax.ShapeDtypeStruct((ranks,) + b...  80.6 us
    pallas_call x1, Pallas kernels, fused_on_device(): pl.pallas_call(place_kernel, out_shape=(jax.ShapeDtypeStruct((rows, width...  6.78 us

profile of v3, /device:TPU:1, one launch (start us, length us, event | category | flops | bytes accessed | tf_op | source)
XLA Modules:
  0.0 89.3 jit_solution(5581072049477275671)
XLA Ops:
  0.6 1.3 %select_reduce_fusion.group_ref = s32[8]{0:T(128)} fusion(s32[8]{0:T(128)} %owner_ref.1), kind=kLoop, calls=%fused_computation | loop fusion | flops 184 | bytes 64 | tf_op jit(solution)/shard_map/reduce_sum | solution.py:614
  1.9 80.6 %adapter_step.1 = (bf16[8,256,768]{2,1,0:T(8,128)(2,1)}, bf16[8,256,768]{2,1,0:T(8,128)(2,1)}, f32[256,768]{1,0:T(8,128)}) custom-call(s32[8]{0:T(128)} %select_reduce_fusion.group_ref, bf16[128,6144]{1,0:T(8,128)(2,1)} %x_hbm.1, bf16[128,6144]{1,0:T(8,128)(2,1)} %g_hbm.1, bf16[128,6144]{1,0:T(8,128)(2,1)} %u_hbm.1, bf16[128,6144]{1,0:T(8,128)(2,1)} %v_hbm.1, ...), custom_call_target="tpu_custom_call" | custom-call | tf_op jit(solution)/shard_map/adapter_step/pallas_call | solution.py:615
  82.5 6.8 %place_groups.1 = (bf16[256,6144]{1,0:T(8,128)(2,1)}, bf16[256,6144]{1,0:T(8,128)(2,1)}, f32[256,768]{1,0:T(8,128)}) custom-call(s32[8]{0:T(128)} %owner_ref.1, bf16[8,256,768]{2,1,0:T(8,128)(2,1)} %get-tuple-element.6.mom_ref, bf16[8,256,768]{2,1,0:T(8,128)(2,1)} %get-tuple-element.7.work_ref, f32[256,768]{1,0:T(8,128)} %get-tuple-element.8.serv_ref), custom_call_target="tpu_custom_call" | custom-call | tf_op jit(solution)/shard_map/place_groups/pallas_call | solution.py:678

commit v4 on v3

--- a/solution.py
+++ b/solution.py
@@ -146,6 +146,8 @@
     out_sem,
     z_send,
     z_recv,
+    zd_send,
+    zd_recv,
     up_send,
     up_recv,
     pre_send,
@@ -226,7 +228,8 @@
         rows = pl.ds(pl.multiple_of(rank * piece, piece), piece)
         if part is None:
             return ups.at[j - 1, rows]
-        return ups.at[j - 1, rows, pl.ds(part * (width // 2), width // 2)]
+        start, size = ((0, width // 4), (width // 4, width // 4), (width // 2, width // 2))[part]
+        return ups.at[j - 1, rows, pl.ds(start, size)]
 
     def z_own(j):
         rows = pl.ds(pl.multiple_of(me * piece, piece), piece)
@@ -241,6 +244,27 @@
             jnp.maximum(sec - 1, 0),
             me,
         )
+
+    def zd_own(j):
+        src = u_hbm.at[
+            pl.ds(pl.multiple_of(diag * piece, piece), piece), pl.ds(width // 2, width // 2)
+        ]
+        return remote(
+            src, up_rows(j, diag, 2), zd_send.at[j - 1], zd_recv.at[j - 1], j - 1, me
+        )
+
+    def zd_pass(j):
+        ref = up_rows(j, diag, 2)
+        return remote(
+            ref, ref, zd_send.at[j - 1], zd_recv.at[j - 1], jnp.maximum(sec - 1, 0), me
+        )
+
+    def zd_step(j):
+        zd_pass(j).wait_recv()
+
+        @pl.when(sec > 0)
+        def _():
+            zd_pass(j).start()
 
     for j in range(1, sections):
 
@@ -331,8 +355,8 @@
     def turn(step, k):
         @pl.when(k <= above)
         def _():
-            if step is z_step:
-                z_step(sec + k)
+            if step in (z_step, zd_step):
+                step(sec + k)
             else:
                 step(*up_args(sec + k))
 
@@ -352,8 +376,16 @@
     dact[...] = contracted(lambda i: g_v[i], v_v)
     turn(spread_pass, 1)
     turn(z_step, 3)
+    for j in range(1, sections):
+
+        @pl.when(sec == j)
+        def _():
+            zd_own(j).start()
+
+    turn(spread_pass, 2)
+    turn(zd_step, 1)
     turn(spread_diag, 1)
-    turn(spread_pass, 2)
+    turn(zd_step, 2)
 
     def cross(k):
         @pl.when(k <= above)
@@ -362,11 +394,12 @@
             slot = sec + k - 1
             mixed[slot] = contracted(lambda i: ups[slot, :, cols_of(i)], v_v)
 
+    turn(spread_pass, 3)
+    turn(zd_step, 3)
     cross(1)
     turn(spread_diag, 2)
-    turn(spread_pass, 3)
+    turn(spread_diag, 3)
     cross(2)
-    turn(spread_diag, 3)
     cross(3)
 
     for k in range(sections - 1, 0, -1):
@@ -459,8 +492,30 @@
     def sib_copy(i):
         return remote(sib_out.at[i], sib_in.at[i], sib_send.at[i], sib_recv.at[i], sec, sib)
 
+    half_rows = rows // 2
+
     def rs_copy(i):
-        return remote(rs_out.at[i], rs_in.at[i], rs_send.at[i], rs_recv.at[i], sec, dests[i])
+        part = pl.ds((i % 2) * half_rows, half_rows)
+        peer = (nbr_x, nbr_y, nbr_x, nbr_x, nbr_y, nbr_y)[i]
+        return remote(
+            rs_out.at[i // 2, part],
+            rs_in.at[i // 2, part],
+            rs_send.at[i],
+            rs_recv.at[i],
+            sec,
+            peer,
+        )
+
+    def carry(arrived, slot):
+        rs_copy(arrived).wait_recv()
+        first = (arrived % 2) * (half_rows // row_step)
+
+        @pl.loop(first, first + half_rows // row_step)
+        def _(k):
+            rs_out[slot, rows_of(k)] = (
+                rs_out[slot, rows_of(k)].astype(jnp.float32)
+                + rs_in[0, rows_of(k)].astype(jnp.float32)
+            ).astype(jnp.bfloat16)
 
     for i, dest in enumerate(dests):
         pack(dest + flip, sib_out.at[i])
@@ -478,18 +533,27 @@
             else:
                 own_sum[rows_of(k)] = both
 
-        if i < 3:
-            rs_copy(i).start()
-
-    for i in range(3):
+        if i == 0:
+            rs_copy(0).start()
+            rs_copy(1).start()
+        if i == 1:
+            rs_copy(2).start()
+        if i == 2:
+            rs_copy(5).start()
+            carry(1, 1)
+            rs_copy(3).start()
+            carry(0, 2)
+            rs_copy(4).start()
+
+    for i in range(2, 6):
         rs_copy(i).wait_recv()
 
     @pl.loop(0, steps)
     def _(k):
         total = own_sum[rows_of(k)]
-        for i in range(3):
+        for i in (1, 2):
             total = total + rs_in[i, rows_of(k)].astype(jnp.float32)
-        comb[rows_of(k)] = total / ranks + se_v[rows_of(k)]
+        comb[rows_of(k)] = total * (1.0 / ranks) + se_v[rows_of(k)]
 
     scale = magnitude(comb)
     inverse = 1.0 / scale
@@ -539,7 +603,7 @@
         spread_drain(*ag_args(t))
     for i in range(4):
         sib_copy(i).wait_send()
-    for i in range(3):
+    for i in range(6):
         rs_copy(i).wait_send()
     for target in range(sections - 1):
 
@@ -552,6 +616,7 @@
         @pl.when(sec == j)
         def _():
             z_own(j).wait_send()
+            zd_own(j).wait_send()
 
         @pl.when(j > sec)
         def _():
@@ -560,6 +625,7 @@
             @pl.when(sec > 0)
             def _():
                 z_pass(j).wait_send()
+                zd_pass(j).wait_send()
 
     for i in range(8):
         keep(i, kept[i]).wait()
@@ -650,14 +716,16 @@
             dma((ranks,)),
             dma((sections - 1,)),
             dma((sections - 1,)),
+            dma((sections - 1,)),
+            dma((sections - 1,)),
             dma((sections - 1, 8)),
             dma((sections - 1, 8)),
             dma((sections - 1,)),
             dma((sections - 1,)),
             dma((4,)),
             dma((4,)),
-            dma((3,)),
-            dma((3,)),
+            dma((6,)),
+            dma((6,)),
             dma((ag_chunks, 8)),
             dma((ag_chunks, 8)),
         ],

time: 89.4 us -> 83.6 us (0.935)
  Pallas kernels: 87.4 us -> 80.8 us
    pallas_call x1, Pallas kernels: 80.6 us -> 74 us  [fused_on_device(): pl.pallas_call(fused_kernel, out_shape=(jax.ShapeDtypeStruct((ranks,) + b...]
where the time goes in v4:
time: 83.6 us; the launch traced here: 82.7 us
  Pallas kernels  80.8 us (97%)
  other arithmetic  1.28 us (2%)
    pallas_call x1, Pallas kernels, fused_on_device(): pl.pallas_call(fused_kernel, out_shape=(jax.ShapeDtypeStruct((ranks,) + b...  74 us
    pallas_call x1, Pallas kernels, fused_on_device(): pl.pallas_call(place_kernel, out_shape=(jax.ShapeDtypeStruct((rows, width...  6.78 us

profile of v4, /device:TPU:1, one launch (start us, length us, event | category | flops | bytes accessed | tf_op | source)
XLA Modules:
  0.0 82.7 jit_solution(3596788317691455594)
XLA Ops:
  0.6 1.3 %select_reduce_fusion.group_ref = s32[8]{0:T(128)} fusion(s32[8]{0:T(128)} %owner_ref.1), kind=kLoop, calls=%fused_computation | loop fusion | flops 184 | bytes 64 | tf_op jit(solution)/shard_map/reduce_sum | solution.py:680
  1.9 74.0 %adapter_step.1 = (bf16[8,256,768]{2,1,0:T(8,128)(2,1)}, bf16[8,256,768]{2,1,0:T(8,128)(2,1)}, f32[256,768]{1,0:T(8,128)}) custom-call(s32[8]{0:T(128)} %select_reduce_fusion.group_ref, bf16[128,6144]{1,0:T(8,128)(2,1)} %x_hbm.1, bf16[128,6144]{1,0:T(8,128)(2,1)} %g_hbm.1, bf16[128,6144]{1,0:T(8,128)(2,1)} %u_hbm.1, bf16[128,6144]{1,0:T(8,128)(2,1)} %v_hbm.1, ...), custom_call_target="tpu_custom_call" | custom-call | tf_op jit(solution)/shard_map/adapter_step/pallas_call | solution.py:681
  75.9 6.8 %place_groups.1 = (bf16[256,6144]{1,0:T(8,128)(2,1)}, bf16[256,6144]{1,0:T(8,128)(2,1)}, f32[256,768]{1,0:T(8,128)}) custom-call(s32[8]{0:T(128)} %owner_ref.1, bf16[8,256,768]{2,1,0:T(8,128)(2,1)} %get-tuple-element.6.mom_ref, bf16[8,256,768]{2,1,0:T(8,128)(2,1)} %get-tuple-element.7.work_ref, f32[256,768]{1,0:T(8,128)} %get-tuple-element.8.serv_ref), custom_call_target="tpu_custom_call" | custom-call | tf_op jit(solution)/shard_map/place_groups/pallas_call | solution.py:746
